TPU v7x, 32 devices: a whole 2x2x4 slice. The times are simulated.
32 devices in a mesh: group: 2 (over x), seq: 16 (over z, y, core).
Axes of the slice: x: 2, y: 2, z: 4, core: 2. Of those that a mesh axis runs over, the one named last changes fastest.
Arguments:
- queries: bfloat16 [4, 2048, 4096], P('group', 'seq'), parts along dimension 0, may hold values from -32 to 32
- key_vectors: bfloat16 [4, 2048, 4096], P('group', 'seq'), parts along dimension 0, may hold values from -24 to 24
- value_vectors: bfloat16 [4, 2048, 4096], P('group', 'seq'), parts along dimension 0, may hold values from -6 to 6
- out_grad: bfloat16 [4, 2048, 4096], P('group', 'seq'), parts along dimension 0, may hold values from -6 to 6
Outputs:
- grad_queries: bfloat16 [4, 2048, 4096], P('group', 'seq'), parts along dimension 0
- grad_keys: bfloat16 [4, 2048, 4096], P('group', 'seq'), parts along dimension 0
- grad_values: bfloat16 [4, 2048, 4096], P('group', 'seq'), parts along dimension 0
There are 2 independent parts, one for each index of `group`. A program takes and returns all parts, laid end to end along the dimension named above; each array names one. Nothing has to cross between parts.
All inputs are finite; a program needn't handle non-finite values.
Results may differ from a plain program's by a relative error of at most 0.0052.
Values may be sent and summed in bfloat16 or wider, within the bound.
A program may use at most 128 MiB of HBM per device.

v0:
```python
import jax
import jax.numpy as jnp
from jax import lax
from jax.sharding import PartitionSpec as P

HEADS = 32


def shortened(array):
    return jax.tree.map(lambda a: a.astype(jnp.bfloat16) if a.dtype == jnp.float32 else a, array)


def item_gradients(operands):
    queries, key_vectors, value_vectors, out_grad = operands
    tokens_all, head_width = queries.shape
    score_scale = head_width ** (-0.5)
    block_rows = min(512, tokens_all)
    grad_keys = jnp.zeros((tokens_all, head_width), jnp.float32)
    grad_values = jnp.zeros((tokens_all, head_width), jnp.float32)
    query_parts = []
    for block_index in range(tokens_all // block_rows):
        row_start = block_index * block_rows
        row_stop = row_start + block_rows
        query_block = queries[row_start:row_stop]
        grad_block = out_grad[row_start:row_stop]
        key_prefix = key_vectors[:row_stop]
        value_prefix = value_vectors[:row_stop]
        scores = (
            jnp.dot(query_block, key_prefix.T, preferred_element_type=jnp.float32) * score_scale
        )
        row_ids = row_start + lax.broadcasted_iota(jnp.int32, (block_rows, row_stop), 0)
        col_ids = lax.broadcasted_iota(jnp.int32, (block_rows, row_stop), 1)
        scores = jnp.where(row_ids >= col_ids, scores, -jnp.inf)
        row_top = jnp.max(scores, axis=1, keepdims=True)
        weights = jnp.exp(scores - row_top)
        softmax_rows = weights / jnp.sum(weights, axis=1, keepdims=True)
        probs_low = softmax_rows.astype(jnp.bfloat16)
        dprobs = jnp.dot(grad_block, value_prefix.T, preferred_element_type=jnp.float32)
        row_delta = jnp.sum(softmax_rows * dprobs, axis=1, keepdims=True)
        dscores = (softmax_rows * (dprobs - row_delta)).astype(jnp.bfloat16)
        value_terms = jnp.dot(probs_low.T, grad_block, preferred_element_type=jnp.float32)
        grad_values = grad_values.at[:row_stop].add(value_terms)
        key_terms = (
            jnp.dot(dscores.T, query_block, preferred_element_type=jnp.float32) * score_scale
        )
        grad_keys = grad_keys.at[:row_stop].add(key_terms)
        query_terms = jnp.dot(dscores, key_prefix, preferred_element_type=jnp.float32) * score_scale
        query_parts.append(query_terms.astype(jnp.bfloat16))
    grad_queries = jnp.concatenate(query_parts, axis=0)
    return (grad_queries, grad_keys.astype(jnp.bfloat16), grad_values.astype(jnp.bfloat16))


def head_gradients(queries, key_vectors, value_vectors, out_grad):
    page_count, tokens_all, local_heads, head_width = queries.shape

    def to_items(operand):
        return jnp.moveaxis(operand, 2, 1).reshape(page_count * local_heads, tokens_all, head_width)

    def from_items(operand):
        return jnp.moveaxis(operand.reshape(page_count, local_heads, tokens_all, head_width), 1, 2)

    results = lax.map(
        item_gradients,
        (to_items(queries), to_items(key_vectors), to_items(value_vectors), to_items(out_grad)),
    )
    return (from_items(results[0]), from_items(results[1]), from_items(results[2]))


def body(queries, key_vectors, value_vectors, out_grad):
    page_count, tok_rows, feature_width = queries.shape
    head_width = feature_width // HEADS
    query_heads = queries.reshape(page_count, tok_rows, HEADS, head_width)
    key_heads = key_vectors.reshape(page_count, tok_rows, HEADS, head_width)
    value_heads = value_vectors.reshape(page_count, tok_rows, HEADS, head_width)
    grad_heads = out_grad.reshape(page_count, tok_rows, HEADS, head_width)
    arrived = (
        lax.all_to_all(query_heads, "seq", split_axis=2, concat_axis=1, tiled=True),
        lax.all_to_all(key_heads, "seq", split_axis=2, concat_axis=1, tiled=True),
        lax.all_to_all(value_heads, "seq", split_axis=2, concat_axis=1, tiled=True),
        lax.all_to_all(grad_heads, "seq", split_axis=2, concat_axis=1, tiled=True),
    )
    results = head_gradients(arrived[0], arrived[1], arrived[2], arrived[3])
    returned = (
        lax.all_to_all(shortened(results[0]), "seq", split_axis=1, concat_axis=2, tiled=True),
        lax.all_to_all(results[1], "seq", split_axis=1, concat_axis=2, tiled=True),
        lax.all_to_all(results[2], "seq", split_axis=1, concat_axis=2, tiled=True),
    )
    return (
        returned[0].reshape(page_count, tok_rows, feature_width),
        returned[1].reshape(page_count, tok_rows, feature_width),
        returned[2].reshape(page_count, tok_rows, feature_width),
    )


def solution(mesh):
    placed = (
        P("group", "seq", None),
        P("group", "seq", None),
        P("group", "seq", None),
        P("group", "seq", None),
    )
    return jax.shard_map(
        body,
        mesh=mesh,
        in_specs=placed,
        out_specs=(P("group", "seq", None), P("group", "seq", None), P("group", "seq", None)),
        check_vma=False,
    )
```

profile of v0, /device:TPU:15, one launch (start us, length us, event | category | flops | bytes accessed | tf_op | source)
XLA Modules:
  0.0 512.6 jit_solution(13454407848001196836)
XLA Ops:
  0.6 3.1 copy.57
  3.8 2.7 copy.58
  6.5 6.6 %all-to-all-start = ((bf16[2,128,32,128]{3,1,0,2:T(8,128)(2,1)}), bf16[2,128,32,128]{3,1,0,2:T(8,128)(2,1)S(1)}, u32[]{:S(2)}, u32[]{:S(2)}) async-start(bf16[2,128,32,128]{3,1,0,2:T(8,128)(2,1)} %copy.58), calls=%async_computation | async-start | bytes 4194304 | tf_op jit(solution)/shard_map/all_to_all | solution.py:77
  13.1 4.1 copy.61
  17.1 4.1 copy.62
  21.2 39.3 %all-to-all-done = bf16[2,128,32,128]{3,1,0,2:T(8,128)(2,1)S(1)} async-done(((bf16[2,128,32,128]{3,1,0,2:T(8,128)(2,1)}), bf16[2,128,32,128]{3,1,0,2:T(8,128)(2,1)S(1)}, u32[]{:S(2)}, u32[]{:S(2)}) %all-to-all-start) | async-done | bytes 2097184 | tf_op jit(solution)/shard_map/all_to_all | solution.py:77
  60.5 4.9 all-to-all-start.1
  65.4 4.1 copy.69
  69.5 4.1 copy.70
  73.5 39.4 %all-to-all-done.1 = bf16[2,128,32,128]{3,1,0,2:T(8,128)(2,1)} async-done(((bf16[2,128,32,128]{3,1,0,2:T(8,128)(2,1)}), bf16[2,128,32,128]{3,1,0,2:T(8,128)(2,1)}, u32[]{:S(2)}, u32[]{:S(2)}) %all-to-all-start.1) | async-done | bytes 2097184 | tf_op jit(solution)/shard_map/all_to_all | solution.py:78
  112.9 4.9 all-to-all-start.3
  117.8 4.1 copy.65
  121.9 4.1 copy.66
  126.0 39.4 %all-to-all-done.3 = bf16[2,128,32,128]{3,1,0,2:T(8,128)(2,1)} async-done(((bf16[2,128,32,128]{3,1,0,2:T(8,128)(2,1)}), bf16[2,128,32,128]{3,1,0,2:T(8,128)(2,1)}, u32[]{:S(2)}, u32[]{:S(2)}) %all-to-all-start.3) | async-done | bytes 2097184 | tf_op jit(solution)/shard_map/all_to_all | solution.py:79
  165.3 4.9 all-to-all-start.2
  173.7 3.1 copy.72
  176.9 40.9 %all-to-all-done.2 = bf16[2,128,32,128]{3,1,0,2:T(8,128)(2,1)} async-done(((bf16[2,128,32,128]{3,1,0,2:T(8,128)(2,1)}), bf16[2,128,32,128]{3,1,0,2:T(8,128)(2,1)}, u32[]{:S(2)}, u32[]{:S(2)}) %all-to-all-start.2) | async-done | bytes 2097184 | tf_op jit(solution)/shard_map/all_to_all | solution.py:80
  217.8 3.2 copy.68
  220.9 121.2 %while.27 = (s32[]{:T(128)}, bf16[4,2048,128]{2,1,0:T(8,128)(2,1)}, bf16[4,2048,128]{2,1,0:T(8,128)(2,1)}, bf16[4,2048,128]{2,1,0:T(8,128)(2,1)}, bf16[4,2048,12...) while((s32[]{:T(128)}, bf16[4,2048,128]{2,1,0:T(8,128)(2,1)}, ...), condition=%wide.region_13.14_spmd, body=%wide.region_0.13_spmd.sunk | while | flops 3407605248 | bytes 125159704 | solution.py:62
  342.1 4.7 copy.79
  346.8 4.9 all-to-all-start.6
  351.8 4.6 copy.73
  356.4 42.8 %all-to-all-done.6 = bf16[2,2048,2,128]{3,2,0,1:T(2,128)(2,1)S(1)} async-done(((bf16[2,2048,2,128]{3,2,0,1:T(2,128)(2,1)}), bf16[2,2048,2,128]{3,2,0,1:T(2,128)(2,1)S(1)}, u32[]{:S(2)}, u32[]{:S(2)}) %all-to-all-start.6) | async-done | bytes 2097184 | tf_op jit(solution)/shard_map/all_to_all | solution.py:86
  399.2 4.9 all-to-all-start.4
  404.1 4.7 copy.76
  408.8 42.8 %all-to-all-done.4 = bf16[2,2048,2,128]{3,2,0,1:T(2,128)(2,1)} async-done(((bf16[2,2048,2,128]{3,2,0,1:T(2,128)(2,1)}), bf16[2,2048,2,128]{3,2,0,1:T(2,128)(2,1)}, u32[]{:S(2)}, u32[]{:S(2)}) %all-to-all-start.4) | async-done | bytes 2097184 | tf_op jit(solution)/shard_map/all_to_all | solution.py:84
  451.6 4.9 all-to-all-start.5
  458.1 3.0 copy.81
  461.2 2.7 copy.84
  468.3 4.1 copy.82
  472.4 31.6 %all-to-all-done.5 = bf16[2,2048,2,128]{3,2,0,1:T(2,128)(2,1)} async-done(((bf16[2,2048,2,128]{3,2,0,1:T(2,128)(2,1)}), bf16[2,2048,2,128]{3,2,0,1:T(2,128)(2,1)}, u32[]{:S(2)}, u32[]{:S(2)}) %all-to-all-start.5) | async-done | bytes 2097184 | tf_op jit(solution)/shard_map/all_to_all | solution.py:85
  508.5 4.1 copy.83
  (162 shorter events, 134.7 us)
Async XLA Ops:
  6.5 54.0 %all-to-all-start = ((bf16[2,128,32,128]{3,1,0,2:T(8,128)(2,1)}), bf16[2,128,32,128]{3,1,0,2:T(8,128)(2,1)S(1)}, u32[]{:S(2)}, u32[]{:S(2)}) async-start(bf16[2,128,32,128]{3,1,0,2:T(8,128)(2,1)} %copy.58), calls=%async_computation | async-start | bytes 4194304 | tf_op jit(solution)/shard_map/all_to_all | solution.py:77
  60.5 52.4 %all-to-all-start.1 = ((bf16[2,128,32,128]{3,1,0,2:T(8,128)(2,1)}), bf16[2,128,32,128]{3,1,0,2:T(8,128)(2,1)}, u32[]{:S(2)}, u32[]{:S(2)}) async-start(bf16[2,128,32,128]{3,1,0,2:T(8,128)(2,1)} %copy.62), calls=%async_computation.1 | async-start | bytes 4194304 | tf_op jit(solution)/shard_map/all_to_all | solution.py:78
  112.9 52.4 %all-to-all-start.3 = ((bf16[2,128,32,128]{3,1,0,2:T(8,128)(2,1)}), bf16[2,128,32,128]{3,1,0,2:T(8,128)(2,1)}, u32[]{:S(2)}, u32[]{:S(2)}) async-start(bf16[2,128,32,128]{3,1,0,2:T(8,128)(2,1)} %copy.70), calls=%async_computation.3 | async-start | bytes 4194304 | tf_op jit(solution)/shard_map/all_to_all | solution.py:79
  165.3 52.4 %all-to-all-start.2 = ((bf16[2,128,32,128]{3,1,0,2:T(8,128)(2,1)}), bf16[2,128,32,128]{3,1,0,2:T(8,128)(2,1)}, u32[]{:S(2)}, u32[]{:S(2)}) async-start(bf16[2,128,32,128]{3,1,0,2:T(8,128)(2,1)} %copy.66), calls=%async_computation.2 | async-start | bytes 4194304 | tf_op jit(solution)/shard_map/all_to_all | solution.py:80
  220.9 1.7 copy-start.1
  222.6 1.6 copy-start
  251.2 1.7 copy-start.1
  252.9 1.6 copy-start
  281.5 1.7 copy-start.1
  283.2 1.6 copy-start
  311.8 1.7 copy-start.1
  313.5 1.6 copy-start
  346.8 52.3 %all-to-all-start.6 = ((bf16[2,2048,2,128]{3,2,0,1:T(2,128)(2,1)}), bf16[2,2048,2,128]{3,2,0,1:T(2,128)(2,1)S(1)}, u32[]{:S(2)}, u32[]{:S(2)}) async-start(bf16[2,2048,2,128]{3,2,0,1:T(2,128)(2,1)} %bitcast.253), calls=%async_computation.6 | async-start | bytes 4194304 | tf_op jit(solution)/shard_map/all_to_all | solution.py:86
  399.2 52.4 %all-to-all-start.4 = ((bf16[2,2048,2,128]{3,2,0,1:T(2,128)(2,1)}), bf16[2,2048,2,128]{3,2,0,1:T(2,128)(2,1)}, u32[]{:S(2)}, u32[]{:S(2)}) async-start(bf16[2,2048,2,128]{3,2,0,1:T(2,128)(2,1)} %bitcast.252), calls=%async_computation.4 | async-start | bytes 4194304 | tf_op jit(solution)/shard_map/all_to_all | solution.py:84
  451.6 52.4 %all-to-all-start.5 = ((bf16[2,2048,2,128]{3,2,0,1:T(2,128)(2,1)}), bf16[2,2048,2,128]{3,2,0,1:T(2,128)(2,1)}, u32[]{:S(2)}, u32[]{:S(2)}) async-start(bf16[2,2048,2,128]{3,2,0,1:T(2,128)(2,1)} %bitcast.251), calls=%async_computation.5 | async-start | bytes 4194304 | tf_op jit(solution)/shard_map/all_to_all | solution.py:85
where the time goes:
time: 515 us; the launch traced here: 513 us
  waiting for transfers between devices  276 us (54%)
  matrix products  91.7 us (18%)
  local copies, waits for them, and re-layouts  84.1 us (16%)
  starting transfers between devices  36 us (7%)
  other arithmetic  23.4 us (5%)
    all_to_all x1, waiting for transfers between devices, body(): lax.all_to_all(shortened(results[0]), 'seq', split_axis=1, concat_axis=2,...  42.8 us
    all_to_all x1, waiting for transfers between devices, body(): lax.all_to_all(results[2], 'seq', split_axis=1, concat_axis=2, tiled=True)  42.8 us
    all_to_all x1, waiting for transfers between devices, body(): lax.all_to_all(grad_heads, 'seq', split_axis=2, concat_axis=1, tiled=True)  40.9 us
    all_to_all x1, waiting for transfers between devices, body(): lax.all_to_all(key_heads, 'seq', split_axis=2, concat_axis=1, tiled=True)  39.4 us
    all_to_all x1, waiting for transfers between devices, body(): lax.all_to_all(value_heads, 'seq', split_axis=2, concat_axis=1, tiled=True)  39.4 us
    all_to_all x1, waiting for transfers between devices, body(): lax.all_to_all(query_heads, 'seq', split_axis=2, concat_axis=1, tiled=True)  39.3 us
    all_to_all x1, waiting for transfers between devices, body(): lax.all_to_all(results[1], 'seq', split_axis=1, concat_axis=2, tiled=True)  31.6 us
    dot_general x16, matrix products, item_gradients(): jnp.dot(dscores.T, query_block, preferred_element_type=jnp.float32)  27 us
  transfers between devices with their start and end apart: 7, of which 7 were waited for; matrix products, arithmetic and copies ran while one was open for 11% of the time, Pallas kernels for 0%

commit v1 on v0

v1 whole, which is shorter than its diff:
```python
import functools

import jax
import jax.numpy as jnp
from jax import lax
from jax.experimental import pallas as pl
from jax.experimental.pallas import tpu as pltpu
from jax.sharding import PartitionSpec as P

HEADS = 32
LOG2_E = 1.4426950408889634


def product(a, b, dims):
    return lax.dot_general(a, b, ((dims[:1], dims[1:]), ((), ())), preferred_element_type=jnp.float32)


def gradient_kernel(in_ref, out_ref, score_buf, dprob_buf, key_sum, value_sum):
    sources, _, rows, width = in_ref.shape
    side = score_buf.shape[1]
    per = side // rows
    blocks = sources // per
    scale = width ** (-0.5)

    def block(which, index):
        return in_ref[pl.ds(index * per, per), which].reshape(side, width)

    key_sum[...] = jnp.zeros_like(key_sum)
    value_sum[...] = jnp.zeros_like(value_sum)

    def row_block(i, carry):
        query = block(0, i)
        grad = block(3, i)

        def scan_keys(j, state, diagonal):
            top, total, dot_total = state
            scores = product(block(1, j), query, (1, 1)) * (scale * LOG2_E)
            if diagonal:
                key_ids = lax.broadcasted_iota(jnp.int32, (side, side), 0)
                query_ids = lax.broadcasted_iota(jnp.int32, (side, side), 1)
                scores = jnp.where(query_ids >= key_ids, scores, -jnp.inf)
            dprobs = product(block(2, j), grad, (1, 1))
            score_buf[j] = scores
            dprob_buf[j] = dprobs
            new_top = jnp.maximum(top, jnp.max(scores, axis=0, keepdims=True))
            weights = jnp.exp2(scores - new_top)
            shrink = jnp.exp2(top - new_top)
            total = total * shrink + jnp.sum(weights, axis=0, keepdims=True)
            dot_total = dot_total * shrink + jnp.sum(weights * dprobs, axis=0, keepdims=True)
            return new_top, total, dot_total

        state = (
            jnp.full((1, side), -jnp.inf, jnp.float32),
            jnp.zeros((1, side), jnp.float32),
            jnp.zeros((1, side), jnp.float32),
        )
        state = lax.fori_loop(0, i, functools.partial(scan_keys, diagonal=False), state)
        top, total, dot_total = scan_keys(i, state, True)
        inverse = 1.0 / total
        row_delta = dot_total * inverse

        def add_terms(j, query_sum):
            probs = jnp.exp2(score_buf[j] - top) * inverse
            dscores = (probs * (dprob_buf[j] - row_delta)).astype(jnp.bfloat16)
            span = pl.ds(pl.multiple_of(j * side, side), side)
            value_sum[span] += product(probs.astype(jnp.bfloat16), grad, (1, 0))
            key_sum[span] += product(dscores, query, (1, 0))
            return query_sum + product(dscores, block(1, j), (0, 0))

        query_sum = lax.fori_loop(0, i + 1, add_terms, jnp.zeros((side, width), jnp.float32))
        out_ref[pl.ds(i * per, per), 0] = (
            (query_sum * scale).astype(jnp.bfloat16).reshape(per, rows, width)
        )
        return carry

    lax.fori_loop(0, blocks, row_block, 0)
    out_ref[:, 1] = (key_sum[...] * scale).astype(jnp.bfloat16).reshape(sources, rows, width)
    out_ref[:, 2] = value_sum[...].astype(jnp.bfloat16).reshape(sources, rows, width)


def page_gradients(arrived, head_width):
    sources, _, rows, features = arrived.shape
    tokens = sources * rows
    side = min(512, tokens)
    heads = features // head_width
    return pl.pallas_call(
        gradient_kernel,
        grid=(heads,),
        in_specs=[pl.BlockSpec((sources, 4, rows, head_width), lambda h: (0, 0, 0, h))],
        out_specs=pl.BlockSpec((sources, 3, rows, head_width), lambda h: (0, 0, 0, h)),
        out_shape=jax.ShapeDtypeStruct((sources, 3, rows, features), jnp.bfloat16),
        scratch_shapes=[
            pltpu.VMEM((tokens // side, side, side), jnp.float32),
            pltpu.VMEM((tokens // side, side, side), jnp.float32),
            pltpu.VMEM((tokens, head_width), jnp.float32),
            pltpu.VMEM((tokens, head_width), jnp.float32),
        ],
        compiler_params=pltpu.CompilerParams(vmem_limit_bytes=56 * 1024 * 1024),
        cost_estimate=pl.CostEstimate(
            flops=heads * 5 * tokens * tokens * head_width * 2,
            bytes_accessed=7 * tokens * features * 2,
            transcendentals=heads * tokens * tokens,
        ),
    )(arrived)


def body(devices, queries, key_vectors, value_vectors, out_grad):
    page_count, rows, feature_width = queries.shape
    head_width = feature_width // HEADS
    part = feature_width // devices
    operands = (queries, key_vectors, value_vectors, out_grad)

    def swap(block):
        return lax.all_to_all(block, "seq", split_axis=0, concat_axis=0, tiled=True)

    pages = []
    for page in range(page_count):
        outgoing = jnp.stack([a[page].reshape(rows, devices, part) for a in operands])
        arrived = swap(jnp.transpose(outgoing, (2, 0, 1, 3)))
        returned = swap(page_gradients(arrived, head_width))
        pages.append(jnp.transpose(returned, (1, 2, 0, 3)).reshape(3, rows, feature_width))
    return tuple(jnp.stack([page[k] for page in pages]) for k in range(3))


def solution(mesh):
    placed = P("group", "seq", None)
    return jax.shard_map(
        functools.partial(body, mesh.shape["seq"]),
        mesh=mesh,
        in_specs=(placed,) * 4,
        out_specs=(placed,) * 3,
        check_vma=False,
    )
```

time: 515 us -> 395 us (0.77)
  matrix products: 91.7 us -> 0 us
  Pallas kernels: 0 us -> 52.3 us
  local copies, waits for them, and re-layouts: 84.1 us -> 56.6 us
  waiting for transfers between devices: 276 us -> 251 us
  starting transfers between devices: 36 us -> 21.3 us
  other arithmetic: 23.4 us -> 11.4 us
    dot_general x80 -> x0, matrix products: 91.7 us -> none  [the longest x16 27 us: item_gradients(): jnp.dot(dscores.T, query_block, preferred_element_type=jnp.float32)]
    pallas_call x0 -> x2, Pallas kernels: none -> 52.3 us  [page_gradients(): pl.pallas_call(gradient_kernel, grid=(heads,), in_specs=[pl.BlockSpec((so...]
    slice x0 -> x12, local copies, waits for them, and re-layouts: none -> 28.8 us  [the longest x8 18.3 us: body(): return tuple((jnp.stack([page[k] for page in pages]) for k in range(3)))]
    all_to_all x7 -> x4, waiting for transfers between devices: 276 us -> 251 us  [swap(): return lax.all_to_all(block, 'seq', split_axis=0, concat_axis=0, tiled=True)]
    all_to_all x10 -> x0, local copies, waits for them, and re-layouts: 23.3 us -> none  [the longest x2 4.63 us: body(): lax.all_to_all(results[2], 'seq', split_axis=1, concat_axis=2, tiled=True)]
    while x19 -> x0, local copies, waits for them, and re-layouts: 19.1 us -> none  [the longest x3 14.1 us: head_gradients(): lax.map(item_gradients, (to_items(queries), to_items(key_vectors), to_ite...]
    reshape x4 -> x0, local copies, waits for them, and re-layouts: 14.9 us -> none  [the longest x1 4.07 us: body(): grad_heads = out_grad.reshape(page_count, tok_rows, HEADS, head_width)]
    all_to_all x7 -> x4, starting transfers between devices: 36 us -> 21.3 us  [swap(): return lax.all_to_all(block, 'seq', split_axis=0, concat_axis=0, tiled=True)]
  transfers between devices with their start and end apart: 7 -> 4, of which waited for: 7 -> 4; matrix products, arithmetic and copies ran while one was open for 11% -> 5% of each run, Pallas kernels for 0% -> 13%
where the time goes in v1:
time: 395 us; the launch traced here: 394 us
  waiting for transfers between devices  251 us (64%)
  local copies, waits for them, and re-layouts  56.6 us (14%)
  Pallas kernels  52.3 us (13%)
  starting transfers between devices  21.3 us (5%)
  other arithmetic  11.4 us (3%)
    all_to_all x4, waiting for transfers between devices, swap(): return lax.all_to_all(block, 'seq', split_axis=0, concat_axis=0, tiled=True)  251 us
    pallas_call x2, Pallas kernels, page_gradients(): pl.pallas_call(gradient_kernel, grid=(heads,), in_specs=[pl.BlockSpec((so...  52.3 us
    all_to_all x4, starting transfers between devices, swap(): return lax.all_to_all(block, 'seq', split_axis=0, concat_axis=0, tiled=True)  21.3 us
    slice x8, local copies, waits for them, and re-layouts, body(): return tuple((jnp.stack([page[k] for page in pages]) for k in range(3)))  18.3 us
    unnamed x23, local copies, waits for them, and re-layouts  18 us
    slice x4, local copies, waits for them, and re-layouts, body(): a[page].reshape(rows, devices, part)  10.5 us
    another operation x8, local copies, waits for them, and re-layouts, body(): jnp.stack([a[page].reshape(rows, devices, part) for a in operands])  9.8 us
  transfers between devices with their start and end apart: 4, of which 4 were waited for; matrix products, arithmetic and copies ran while one was open for 5% of the time, Pallas kernels for 13%

profile of v1, /device:TPU:15, one launch (start us, length us, event | category | flops | bytes accessed | tf_op | source)
XLA Modules:
  0.0 393.7 jit_solution(10864850628624328401)
XLA Ops:
  0.6 1.7 fusion.2
  4.3 2.7 fusion.3
  7.0 1.6 copy.33
  9.9 3.1 fusion.4
  13.0 1.6 copy.34
  15.9 3.1 fusion.5
  19.0 1.6 copy.35
  21.9 3.7 maximum_bitcast_fusion
  25.7 6.6 %all-to-all-start = ((bf16[16,4,128,256]{3,2,1,0:T(8,128)(2,1)}), bf16[16,4,128,256]{3,2,1,0:T(8,128)(2,1)}, u32[]{:S(2)}, u32[]{:S(2)}) async-start(bf16[16,4,128,256]{3,2,1,0:T(8,128)(2,1)} %maximum_bitcast_fusion), calls=%async_computation | async-start | bytes 8388608 | tf_op jit(solution)/shard_map/all_to_all | solution.py:114
  39.5 3.4 maximum_bitcast_fusion.1
  42.9 81.8 %all-to-all-done.in_ref = bf16[16,4,128,256]{3,2,1,0:T(8,128)(2,1)} async-done(((bf16[16,4,128,256]{3,2,1,0:T(8,128)(2,1)}), bf16[16,4,128,256]{3,2,1,0:T(8,128)(2,1)}, u32[]{:S(2)}, u32[]{:S(2)}) %all-to-all-start) | async-done | bytes 4194336 | tf_op jit(solution)/shard_map/all_to_all | solution.py:114
  124.7 4.9 %all-to-all-start.2 = ((bf16[16,4,128,256]{3,2,1,0:T(8,128)(2,1)}), bf16[16,4,128,256]{3,2,1,0:T(8,128)(2,1)}, u32[]{:S(2)}, u32[]{:S(2)}) async-start(bf16[16,4,128,256]{3,2,1,0:T(8,128)(2,1)} %maximum_bitcast_fusion.1), calls=%async_computation.2 | async-start | bytes 8388608 | tf_op jit(solution)/shard_map/all_to_all | solution.py:114
  129.6 26.1 %shard_map.67 = bf16[16,3,128,256]{3,2,1,0:T(8,128)(2,1)} custom-call(bf16[16,4,128,256]{3,2,1,0:T(8,128)(2,1)} %all-to-all-done.in_ref), custom_call_target="tpu_custom_call" | custom-call | flops 10737418240 | bytes 7340032 | tf_op jit(solution)/shard_map/pallas_call | solution.py:86
  155.7 66.3 %all-to-all-done.2.in_ref = bf16[16,4,128,256]{3,2,1,0:T(8,128)(2,1)} async-done(((bf16[16,4,128,256]{3,2,1,0:T(8,128)(2,1)}), bf16[16,4,128,256]{3,2,1,0:T(8,128)(2,1)}, u32[]{:S(2)}, u32[]{:S(2)}) %all-to-all-start.2) | async-done | bytes 4194336 | tf_op jit(solution)/shard_map/all_to_all | solution.py:114
  222.1 4.9 %all-to-all-start.1 = ((bf16[16,3,128,256]{3,2,1,0:T(8,128)(2,1)}), bf16[16,3,128,256]{3,2,1,0:T(8,128)(2,1)S(1)}, u32[]{:S(2)}, u32[]{:S(2)}) async-start(bf16[16,3,128,256]{3,2,1,0:T(8,128)(2,1)} %shard_map.67), calls=%async_computation.1 | async-start | bytes 6291456 | tf_op jit(solution)/shard_map/all_to_all | solution.py:114
  227.0 26.1 %shard_map.68 = bf16[16,3,128,256]{3,2,1,0:T(8,128)(2,1)} custom-call(bf16[16,4,128,256]{3,2,1,0:T(8,128)(2,1)} %all-to-all-done.2.in_ref), custom_call_target="tpu_custom_call" | custom-call | flops 10737418240 | bytes 7340032 | tf_op jit(solution)/shard_map/pallas_call | solution.py:86
  253.1 43.7 %all-to-all-done.1 = bf16[16,3,128,256]{3,2,1,0:T(8,128)(2,1)S(1)} async-done(((bf16[16,3,128,256]{3,2,1,0:T(8,128)(2,1)}), bf16[16,3,128,256]{3,2,1,0:T(8,128)(2,1)S(1)}, u32[]{:S(2)}, u32[]{:S(2)}) %all-to-all-start.1) | async-done | bytes 3145760 | tf_op jit(solution)/shard_map/all_to_all | solution.py:114
  296.9 1.6 copy-done
  298.5 4.9 %all-to-all-start.3 = ((bf16[16,3,128,256]{3,2,1,0:T(8,128)(2,1)}), bf16[16,3,128,256]{3,2,1,0:T(8,128)(2,1)S(1)}, u32[]{:S(2)}, u32[]{:S(2)}) async-start(bf16[16,3,128,256]{3,2,1,0:T(8,128)(2,1)} %shard_map.68), calls=%async_computation.3 | async-start | bytes 6291456 | tf_op jit(solution)/shard_map/all_to_all | solution.py:114
  303.4 3.6 fusion
  307.0 2.3 copy.27
  309.3 2.3 copy.25
  311.6 2.3 copy.15
  313.9 59.5 %all-to-all-done.3 = bf16[16,3,128,256]{3,2,1,0:T(8,128)(2,1)S(1)} async-done(((bf16[16,3,128,256]{3,2,1,0:T(8,128)(2,1)}), bf16[16,3,128,256]{3,2,1,0:T(8,128)(2,1)S(1)}, u32[]{:S(2)}, u32[]{:S(2)}) %all-to-all-start.3) | async-done | bytes 3145760 | tf_op jit(solution)/shard_map/all_to_all | solution.py:114
  373.3 1.7 fusion.1
  375.0 1.6 copy.28
  376.7 1.4 pad_maximum_fusion.2
  378.1 2.7 copy.31
  380.8 2.3 copy.26
  384.5 2.7 copy.30
  387.2 2.3 copy.24
  391.0 2.7 copy.29
  (26 shorter events, 16.0 us)
Async XLA Ops:
  25.7 99.0 %all-to-all-start = ((bf16[16,4,128,256]{3,2,1,0:T(8,128)(2,1)}), bf16[16,4,128,256]{3,2,1,0:T(8,128)(2,1)}, u32[]{:S(2)}, u32[]{:S(2)}) async-start(bf16[16,4,128,256]{3,2,1,0:T(8,128)(2,1)} %maximum_bitcast_fusion), calls=%async_computation | async-start | bytes 8388608 | tf_op jit(solution)/shard_map/all_to_all | solution.py:114
  32.9 3.4 copy-start.1
  34.9 3.3 copy-start.2
  38.2 1.2 copy-start.5
  124.7 97.4 %all-to-all-start.2 = ((bf16[16,4,128,256]{3,2,1,0:T(8,128)(2,1)}), bf16[16,4,128,256]{3,2,1,0:T(8,128)(2,1)}, u32[]{:S(2)}, u32[]{:S(2)}) async-start(bf16[16,4,128,256]{3,2,1,0:T(8,128)(2,1)} %maximum_bitcast_fusion.1), calls=%async_computation.2 | async-start | bytes 8388608 | tf_op jit(solution)/shard_map/all_to_all | solution.py:114
  222.1 74.8 %all-to-all-start.1 = ((bf16[16,3,128,256]{3,2,1,0:T(8,128)(2,1)}), bf16[16,3,128,256]{3,2,1,0:T(8,128)(2,1)S(1)}, u32[]{:S(2)}, u32[]{:S(2)}) async-start(bf16[16,3,128,256]{3,2,1,0:T(8,128)(2,1)} %shard_map.67), calls=%async_computation.1 | async-start | bytes 6291456 | tf_op jit(solution)/shard_map/all_to_all | solution.py:114
  296.9 1.6 copy-start
  298.5 74.8 %all-to-all-start.3 = ((bf16[16,3,128,256]{3,2,1,0:T(8,128)(2,1)}), bf16[16,3,128,256]{3,2,1,0:T(8,128)(2,1)S(1)}, u32[]{:S(2)}, u32[]{:S(2)}) async-start(bf16[16,3,128,256]{3,2,1,0:T(8,128)(2,1)} %shard_map.68), calls=%async_computation.3 | async-start | bytes 6291456 | tf_op jit(solution)/shard_map/all_to_all | solution.py:114
  378.1 5.0 %copy-start.4 = (bf16[1,128,16,256]{1,3,2,0:T(8,128)(2,1)S(1)}, bf16[1,128,16,256]{1,3,2,0:T(8,128)(2,1)}, u32[]{:S(2)}) copy-start(bf16[1,128,16,256]{1,3,2,0:T(8,128)(2,1)} %copy.25) | copy-start | bytes 3145732
  384.5 5.0 %copy-start.3 = (bf16[1,128,16,256]{1,3,2,0:T(8,128)(2,1)S(1)}, bf16[1,128,16,256]{1,3,2,0:T(8,128)(2,1)}, u32[]{:S(2)}) copy-start(bf16[1,128,16,256]{1,3,2,0:T(8,128)(2,1)} %copy.15) | copy-start | bytes 3145732

commit v2 on v1

v2 whole, which is shorter than its diff:
```python
import functools

import jax
import jax.numpy as jnp
from jax import lax
from jax.experimental import pallas as pl
from jax.experimental.pallas import tpu as pltpu
from jax.sharding import PartitionSpec as P

HEADS = 32
LOG2_E = 1.4426950408889634


def product(a, b, dims):
    return lax.dot_general(a, b, ((dims[:1], dims[1:]), ((), ())), preferred_element_type=jnp.float32)


def gradient_kernel(later_ref, kv_ref, qg_ref, prefix_ref, dq_ref, dkv_ref, dprefix_ref, score_buf, dprob_buf, key_sum, value_sum):
    sources, _, rows, width = kv_ref.shape
    side = score_buf.shape[1]
    per = side // rows
    blocks = sources // per
    scale = width ** (-0.5)
    skipped = (1 - later_ref[0]) * blocks

    def block(ref, which, index):
        return ref[pl.ds(index * per, per), which].reshape(side, width)

    key_sum[...] = jnp.zeros_like(key_sum)
    value_sum[...] = jnp.zeros_like(value_sum)

    def row_block(i, carry):
        query = block(qg_ref, 0, i)
        grad = block(qg_ref, 1, i)

        def scan_keys(j, state, source, offset, diagonal):
            top, total, dot_total = state
            scores = product(block(source, 0, j), query, (1, 1)) * (scale * LOG2_E)
            if diagonal:
                key_ids = lax.broadcasted_iota(jnp.int32, (side, side), 0)
                query_ids = lax.broadcasted_iota(jnp.int32, (side, side), 1)
                scores = jnp.where(query_ids >= key_ids, scores, -jnp.inf)
            dprobs = product(block(source, 1, j), grad, (1, 1))
            score_buf[offset + j] = scores
            dprob_buf[offset + j] = dprobs
            new_top = jnp.maximum(top, jnp.max(scores, axis=0, keepdims=True))
            weights = jnp.exp2(scores - new_top)
            shrink = jnp.exp2(top - new_top)
            total = total * shrink + jnp.sum(weights, axis=0, keepdims=True)
            dot_total = dot_total * shrink + jnp.sum(weights * dprobs, axis=0, keepdims=True)
            return new_top, total, dot_total

        state = (
            jnp.full((1, side), -jnp.inf, jnp.float32),
            jnp.zeros((1, side), jnp.float32),
            jnp.zeros((1, side), jnp.float32),
        )
        own = functools.partial(scan_keys, source=kv_ref, offset=blocks)
        earlier = functools.partial(scan_keys, source=prefix_ref, offset=0, diagonal=False)
        state = own(i, state, diagonal=True)
        state = lax.fori_loop(0, i, functools.partial(own, diagonal=False), state)
        top, total, dot_total = lax.fori_loop(skipped, blocks, earlier, state)
        inverse = 1.0 / total
        row_delta = dot_total * inverse

        def add_terms(j, query_sum, source, offset):
            slot = offset + j
            probs = jnp.exp2(score_buf[slot] - top) * inverse
            dscores = (probs * (dprob_buf[slot] - row_delta)).astype(jnp.bfloat16)
            span = pl.ds(pl.multiple_of(slot * side, side), side)
            value_sum[span] += product(probs.astype(jnp.bfloat16), grad, (1, 0))
            key_sum[span] += product(dscores, query, (1, 0))
            return query_sum + product(dscores, block(source, 0, j), (0, 0))

        query_sum = jnp.zeros((side, width), jnp.float32)
        query_sum = lax.fori_loop(
            0, i + 1, functools.partial(add_terms, source=kv_ref, offset=blocks), query_sum
        )
        query_sum = lax.fori_loop(
            skipped, blocks, functools.partial(add_terms, source=prefix_ref, offset=0), query_sum
        )
        dq_ref[pl.ds(i * per, per), 0] = (
            (query_sum * scale).astype(jnp.bfloat16).reshape(per, rows, width)
        )
        return carry

    lax.fori_loop(0, blocks, row_block, 0)
    half = sources * rows
    for start, ref in ((0, dprefix_ref), (half, dkv_ref)):
        span = pl.ds(start, half)
        ref[:, 0] = (key_sum[span] * scale).astype(jnp.bfloat16).reshape(sources, rows, width)
        ref[:, 1] = value_sum[span].astype(jnp.bfloat16).reshape(sources, rows, width)


def page_gradients(later, kv, qg, prefix, head_width):
    sources, _, rows, features = kv.shape
    half = sources * rows
    side = min(512, half)
    heads = features // head_width

    def spec(kinds):
        return pl.BlockSpec((sources, kinds, rows, head_width), lambda h: (0, 0, 0, h))

    def shape(kinds):
        return jax.ShapeDtypeStruct((sources, kinds, rows, features), jnp.bfloat16)

    return pl.pallas_call(
        gradient_kernel,
        grid=(heads,),
        in_specs=[pl.BlockSpec(memory_space=pltpu.SMEM), spec(2), spec(2), spec(2)],
        out_specs=[spec(1), spec(2), spec(2)],
        out_shape=[shape(1), shape(2), shape(2)],
        scratch_shapes=[
            pltpu.VMEM((2 * half // side, side, side), jnp.float32),
            pltpu.VMEM((2 * half // side, side, side), jnp.float32),
            pltpu.VMEM((2 * half, head_width), jnp.float32),
            pltpu.VMEM((2 * half, head_width), jnp.float32),
        ],
        compiler_params=pltpu.CompilerParams(vmem_limit_bytes=56 * 1024 * 1024),
        cost_estimate=pl.CostEstimate(
            flops=heads * 15 * half * half * head_width * 2,
            bytes_accessed=11 * half * features * 2,
            transcendentals=heads * 3 * half * half,
        ),
    )(later, kv, qg, prefix)


def pack_kernel(first_ref, second_ref, out_ref):
    out_ref[0, 0] = first_ref[0]
    out_ref[0, 1] = second_ref[0]


def pack(page, owners, first, second):
    rows, width = first.shape[1:]
    part = width // owners
    source = pl.BlockSpec((1, rows, part), lambda o: (page, 0, o))
    return pl.pallas_call(
        pack_kernel,
        grid=(owners,),
        in_specs=[source, source],
        out_specs=pl.BlockSpec((1, 2, rows, part), lambda o: (o, 0, 0, 0)),
        out_shape=jax.ShapeDtypeStruct((owners, 2, rows, part), jnp.bfloat16),
        cost_estimate=pl.CostEstimate(flops=0, bytes_accessed=8 * rows * width, transcendentals=0),
    )(first, second)


def unpack_kernel(page_count, *refs):
    query_refs, kv_refs = refs[:page_count], refs[page_count : 2 * page_count]
    dq_ref, dk_ref, dv_ref = refs[2 * page_count :]
    for page in range(page_count):
        dq_ref[page] = query_refs[page][0, 0]
        dk_ref[page] = kv_refs[page][0, 0]
        dv_ref[page] = kv_refs[page][0, 1]


def unpack(query_parts, kv_parts):
    page_count = len(query_parts)
    owners, _, rows, part = query_parts[0].shape
    spec = lambda kinds: pl.BlockSpec((1, kinds, rows, part), lambda o: (o, 0, 0, 0))
    result = jax.ShapeDtypeStruct((page_count, rows, owners * part), jnp.bfloat16)
    return pl.pallas_call(
        functools.partial(unpack_kernel, page_count),
        grid=(owners,),
        in_specs=[spec(1)] * page_count + [spec(2)] * page_count,
        out_specs=[pl.BlockSpec((page_count, rows, part), lambda o: (0, 0, o))] * 3,
        out_shape=[result] * 3,
    )(*query_parts, *kv_parts)


def body(devices, queries, key_vectors, value_vectors, out_grad):
    page_count, rows, feature_width = queries.shape
    head_width = feature_width // HEADS
    owners = devices // 2
    halves = [list(range(owners)), list(range(owners, devices))]
    upward = [(i, i + owners) for i in range(owners)]
    downward = [(i + owners, i) for i in range(owners)]
    later = (lax.axis_index("seq") // owners).astype(jnp.int32).reshape(1)

    def swap(block):
        return lax.all_to_all(
            block, "seq", split_axis=0, concat_axis=0, axis_index_groups=halves, tiled=True
        )

    query_parts, kv_parts = [], []
    for page in range(page_count):
        kv = swap(pack(page, owners, key_vectors, value_vectors))
        prefix = lax.ppermute(kv, "seq", upward)
        qg = swap(pack(page, owners, queries, out_grad))
        dq, dkv, dprefix = page_gradients(later, kv, qg, prefix, head_width)
        back = lax.ppermute(dprefix, "seq", downward)
        query_parts.append(swap(dq))
        total = dkv.astype(jnp.float32) + back.astype(jnp.float32)
        kv_parts.append(swap(total.astype(jnp.bfloat16)))
    return tuple(unpack(query_parts, kv_parts))


def solution(mesh):
    placed = P("group", "seq", None)
    return jax.shard_map(
        functools.partial(body, mesh.shape["seq"]),
        mesh=mesh,
        in_specs=(placed,) * 4,
        out_specs=(placed,) * 3,
        check_vma=False,
    )
```

time: 395 us -> 524 us (1.33)
  starting transfers between devices: 21.3 us -> 83.5 us
  blocking collectives: 0 us -> 56.8 us
  local copies, waits for them, and re-layouts: 56.6 us -> 1.02 us
  waiting for transfers between devices: 251 us -> 306 us
  Pallas kernels: 52.3 us -> 64.4 us
    ppermute x0 -> x4, waiting for transfers between devices: none -> 252 us  [the longest x2 152 us: body(): prefix = lax.ppermute(kv, 'seq', upward)]
    all_to_all x4 -> x7, waiting for transfers between devices: 251 us -> 54 us  [swap(): lax.all_to_all(block, 'seq', split_axis=0, concat_axis=0, axis_index_grou...]
    all_to_all x0 -> x1, blocking collectives: none -> 56.8 us  [swap(): lax.all_to_all(block, 'seq', split_axis=0, concat_axis=0, axis_index_grou...]
    all_to_all x4 -> x7, starting transfers between devices: 21.3 us -> 72.7 us  [swap(): lax.all_to_all(block, 'seq', split_axis=0, concat_axis=0, axis_index_grou...]
    slice x12 -> x0, local copies, waits for them, and re-layouts: 28.8 us -> none  [the longest x8 18.3 us: body(): return tuple((jnp.stack([page[k] for page in pages]) for k in range(3)))]
    unnamed x23 -> x10, local copies, waits for them, and re-layouts: 18 us -> 1.02 us
    pallas_call x2 -> x7, Pallas kernels: 52.3 us -> 64.4 us  [the longest x2 33.7 us: page_gradients(): pl.pallas_call(gradient_kernel, grid=(heads,), in_specs=[pl.BlockSpec(mem...]
    ppermute x0 -> x4, starting transfers between devices: none -> 10.8 us  [the longest x2 8.22 us: body(): prefix = lax.ppermute(kv, 'seq', upward)]
  transfers between devices with their start and end apart: 4 -> 11, of which waited for: 4 -> 7; matrix products, arithmetic and copies ran while one was open for 5% -> 1% of each run, Pallas kernels for 13% -> 10%
where the time goes in v2:
time: 524 us; the launch traced here: 520 us
  waiting for transfers between devices  306 us (58%)
  starting transfers between devices  83.5 us (16%)
  Pallas kernels  64.4 us (12%)
  blocking collectives  56.8 us (11%)
  other arithmetic  7.78 us (1%)
    ppermute x2, waiting for transfers between devices, body(): prefix = lax.ppermute(kv, 'seq', upward)  152 us
    ppermute x2, waiting for transfers between devices, body(): back = lax.ppermute(dprefix, 'seq', downward)  100 us
    all_to_all x7, starting transfers between devices, swap(): lax.all_to_all(block, 'seq', split_axis=0, concat_axis=0, axis_index_grou...  72.7 us
    all_to_all x1, blocking collectives, swap(): lax.all_to_all(block, 'seq', split_axis=0, concat_axis=0, axis_index_grou...  56.8 us
    all_to_all x7, waiting for transfers between devices, swap(): lax.all_to_all(block, 'seq', split_axis=0, concat_axis=0, axis_index_grou...  54 us
    pallas_call x2, Pallas kernels, page_gradients(): pl.pallas_call(gradient_kernel, grid=(heads,), in_specs=[pl.BlockSpec(mem...  33.7 us
    pallas_call x4, Pallas kernels, pack(): pl.pallas_call(pack_kernel, grid=(owners,), in_specs=[source, source], ou...  23 us
  transfers between devices with their start and end apart: 11, of which 7 were waited for; matrix products, arithmetic and copies ran while one was open for 1% of the time, Pallas kernels for 10%

profile of v2, /device:TPU:15, one launch (start us, length us, event | category | flops | bytes accessed | tf_op | source)
XLA Modules:
  0.0 520.4 jit_solution(11725679452692842655)
XLA Ops:
  0.6 5.7 %shard_map.70 = bf16[8,2,128,512]{3,2,1,0:T(8,128)(2,1)} custom-call(bf16[2,128,4096]{2,1,0:T(8,128)(2,1)} %first_ref.6, bf16[2,128,4096]{2,1,0:T(8,128)(2,1)} %second_ref.6), custom_call_target="tpu_custom_call" | custom-call | bytes 4194304 | tf_op jit(solution)/shard_map/pallas_call | solution.py:137
  6.4 4.5 all-to-all-start.3
  10.9 5.7 %shard_map.71 = bf16[8,2,128,512]{3,2,1,0:T(8,128)(2,1)} custom-call(bf16[2,128,4096]{2,1,0:T(8,128)(2,1)} %first_ref.7, bf16[2,128,4096]{2,1,0:T(8,128)(2,1)} %second_ref.7), custom_call_target="tpu_custom_call" | custom-call | bytes 4194304 | tf_op jit(solution)/shard_map/pallas_call | solution.py:137
  16.6 18.0 %all-to-all-done.3.kv_ref = bf16[8,2,128,512]{3,2,1,0:T(8,128)(2,1)S(1)} async-done(((bf16[8,2,128,512]{3,2,1,0:T(8,128)(2,1)}), bf16[8,2,128,512]{3,2,1,0:T(8,128)(2,1)S(1)}, u32[]{:S(2)}, u32[]{:S(2)}) %all-to-all-start.3) | async-done | bytes 2097184 | tf_op jit(solution)/shard_map/all_to_all | solution.py:180
  34.6 6.2 %all-to-all-start.4 = ((bf16[8,2,128,512]{3,2,1,0:T(8,128)(2,1)}), bf16[8,2,128,512]{3,2,1,0:T(8,128)(2,1)}, u32[]{:S(2)}, u32[]{:S(2)}) async-start(bf16[8,2,128,512]{3,2,1,0:T(8,128)(2,1)} %shard_map.71), calls=%async_computation.4 | async-start | bytes 4194304 | tf_op jit(solution)/shard_map/all_to_all | solution.py:180
  40.9 5.7 %shard_map.67 = bf16[8,2,128,512]{3,2,1,0:T(8,128)(2,1)} custom-call(bf16[2,128,4096]{2,1,0:T(8,128)(2,1)} %first_ref.6, bf16[2,128,4096]{2,1,0:T(8,128)(2,1)} %second_ref.6), custom_call_target="tpu_custom_call" | custom-call | bytes 4194304 | tf_op jit(solution)/shard_map/pallas_call | solution.py:137
  46.6 18.1 %all-to-all-done.4.qg_ref = bf16[8,2,128,512]{3,2,1,0:T(8,128)(2,1)} async-done(((bf16[8,2,128,512]{3,2,1,0:T(8,128)(2,1)}), bf16[8,2,128,512]{3,2,1,0:T(8,128)(2,1)}, u32[]{:S(2)}, u32[]{:S(2)}) %all-to-all-start.4) | async-done | bytes 2097184 | tf_op jit(solution)/shard_map/all_to_all | solution.py:180
  64.7 5.5 %all-to-all-start = ((bf16[8,2,128,512]{3,2,1,0:T(8,128)(2,1)}), bf16[8,2,128,512]{3,2,1,0:T(8,128)(2,1)S(1)}, u32[]{:S(2)}, u32[]{:S(2)}) async-start(bf16[8,2,128,512]{3,2,1,0:T(8,128)(2,1)} %shard_map.67), calls=%async_computation | async-start | bytes 4194304 | tf_op jit(solution)/shard_map/all_to_all | solution.py:180
  70.2 5.7 %shard_map.68 = bf16[8,2,128,512]{3,2,1,0:T(8,128)(2,1)} custom-call(bf16[2,128,4096]{2,1,0:T(8,128)(2,1)} %first_ref.7, bf16[2,128,4096]{2,1,0:T(8,128)(2,1)} %second_ref.7), custom_call_target="tpu_custom_call" | custom-call | bytes 4194304 | tf_op jit(solution)/shard_map/pallas_call | solution.py:137
  75.9 18.0 %all-to-all-done.kv_ref = bf16[8,2,128,512]{3,2,1,0:T(8,128)(2,1)S(1)} async-done(((bf16[8,2,128,512]{3,2,1,0:T(8,128)(2,1)}), bf16[8,2,128,512]{3,2,1,0:T(8,128)(2,1)S(1)}, u32[]{:S(2)}, u32[]{:S(2)}) %all-to-all-start) | async-done | bytes 2097184 | tf_op jit(solution)/shard_map/all_to_all | solution.py:180
  93.9 6.3 %all-to-all-start.1 = ((bf16[8,2,128,512]{3,2,1,0:T(8,128)(2,1)}), bf16[8,2,128,512]{3,2,1,0:T(8,128)(2,1)}, u32[]{:S(2)}, u32[]{:S(2)}) async-start(bf16[8,2,128,512]{3,2,1,0:T(8,128)(2,1)} %shard_map.68), calls=%async_computation.1 | async-start | bytes 4194304 | tf_op jit(solution)/shard_map/all_to_all | solution.py:180
  100.2 5.6 %collective-permute-start.1 = (bf16[8,2,128,512]{3,2,1,0:T(8,128)(2,1)}, bf16[8,2,128,512]{3,2,1,0:T(8,128)(2,1)}, u32[]{:S(2)}, u32[]{:S(2)}) collective-permute-start(bf16[8,2,128,512]{3,2,1,0:T(8,128)(2,1)} %copy-done.4), channel_id=1, source_target_pairs={{0,8},{1,9},{2,10},{3,11},{4,12},{5,13},{6,14},{7,15},{16,24},{17,... | collective-permute-start | bytes 6291464 | tf_op jit(solution)/shard_map/ppermute | solution.py:187
  105.7 2.7 collective-permute-start
  108.4 130.9 %collective-permute-done.1.prefix_ref = bf16[8,2,128,512]{3,2,1,0:T(8,128)(2,1)} collective-permute-done((bf16[8,2,128,512]{3,2,1,0:T(8,128)(2,1)}, bf16[8,2,128,512]{3,2,1,0:T(8,128)(2,1)}, u32[]{:S(2)}, u32[]{:S(2)}) %collective-permute-start.1) | collective-permute-done | bytes 2097184 | tf_op jit(solution)/shard_map/ppermute | solution.py:187
  239.2 16.9 %shard_map.72 = (bf16[8,1,128,512]{3,2,1,0:T(8,128)(2,1)}, bf16[8,2,128,512]{3,2,1,0:T(8,128)(2,1)}, bf16[8,2,128,512]{3,2,1,0:T(8,128)(2,1)}) custom-call(s32[1]{0:T(128)} %bitcast.later_ref, bf16[8,2,128,512]{3,2,1,0:T(8,128)(2,1)} %copy-done.4, bf16[8,2,128,512]{3,2,1,0:T(8,128)(2,1)} %all-to-all-done.4.qg_ref, ...), custom_call_target="tpu_custom_call" | custom-call | flops 16106127360 | bytes 11534336 | tf_op jit(solution)/shard_map/pallas_call | solution.py:107
  256.1 0.0 all-to-all-done.1.qg_ref
  256.2 5.8 %all-to-all-start.5 = ((bf16[8,1,128,512]{3,2,1,0:T(8,128)(2,1)}), bf16[8,1,128,512]{3,2,1,0:T(8,128)(2,1)S(1)}, u32[]{:S(2)}, u32[]{:S(2)}) async-start(bf16[8,1,128,512]{3,2,1,0:T(8,128)(2,1)} %get-tuple-element.10), calls=%async_computation.5 | async-start | bytes 2097152 | tf_op jit(solution)/shard_map/all_to_all | solution.py:180
  262.0 1.3 collective-permute-start.3
  263.3 20.9 %collective-permute-done.prefix_ref = bf16[8,2,128,512]{3,2,1,0:T(8,128)(2,1)} collective-permute-done((bf16[8,2,128,512]{3,2,1,0:T(8,128)(2,1)S(1)}, bf16[8,2,128,512]{3,2,1,0:T(8,128)(2,1)}, u32[]{:S(2)}, u32[]{:S(2)}) %collective-permute-start) | collective-permute-done | bytes 2097184 | tf_op jit(solution)/shard_map/ppermute | solution.py:187
  284.1 16.8 %shard_map.69 = (bf16[8,1,128,512]{3,2,1,0:T(8,128)(2,1)}, bf16[8,2,128,512]{3,2,1,0:T(8,128)(2,1)}, bf16[8,2,128,512]{3,2,1,0:T(8,128)(2,1)}) custom-call(s32[1]{0:T(128)} %bitcast.later_ref, bf16[8,2,128,512]{3,2,1,0:T(8,128)(2,1)} %copy-done.3, bf16[8,2,128,512]{3,2,1,0:T(8,128)(2,1)} %all-to-all-done.1.qg_ref, ...), custom_call_target="tpu_custom_call" | custom-call | flops 16106127360 | bytes 11534336 | tf_op jit(solution)/shard_map/pallas_call | solution.py:107
  301.0 0.0 all-to-all-done.5.refs_1_
  301.0 5.0 all-to-all-start.2
  306.0 34.0 %collective-permute-done.3 = bf16[8,2,128,512]{3,2,1,0:T(8,128)(2,1)} collective-permute-done((bf16[8,2,128,512]{3,2,1,0:T(8,128)(2,1)}, bf16[8,2,128,512]{3,2,1,0:T(8,128)(2,1)}, u32[]{:S(2)}, u32[]{:S(2)}) %collective-permute-start.3) | collective-permute-done | bytes 2097184 | tf_op jit(solution)/shard_map/ppermute | solution.py:190
  340.0 4.2 add_convert_fusion
  344.2 0.0 all-to-all-done.2.refs_0_
  344.2 1.0 copy-done.2
  345.2 39.3 %all-to-all-start.7 = ((bf16[8,2,128,512]{3,2,1,0:T(8,128)(2,1)}), bf16[8,2,128,512]{3,2,1,0:T(8,128)(2,1)S(1)}, u32[]{:S(2)}, u32[]{:S(2)}) async-start(bf16[8,2,128,512]{3,2,1,0:T(8,128)(2,1)} %add_convert_fusion), calls=%async_computation.7 | async-start | bytes 4194304 | tf_op jit(solution)/shard_map/all_to_all | solution.py:180
  384.6 1.3 collective-permute-start.2
  385.9 66.4 %collective-permute-done.2 = bf16[8,2,128,512]{3,2,1,0:T(8,128)(2,1)S(1)} collective-permute-done((bf16[8,2,128,512]{3,2,1,0:T(8,128)(2,1)}, bf16[8,2,128,512]{3,2,1,0:T(8,128)(2,1)S(1)}, u32[]{:S(2)}, u32[]{:S(2)}) %collective-permute-start.2) | collective-permute-done | bytes 2097184 | tf_op jit(solution)/shard_map/ppermute | solution.py:190
  452.3 3.6 add_convert_fusion.1
  455.8 56.8 %all_to_all.40.refs_2_ = bf16[8,2,128,512]{3,2,1,0:T(8,128)(2,1)} all-to-all(bf16[8,2,128,512]{3,2,1,0:T(8,128)(2,1)} %add_convert_fusion.1), channel_id=1, replica_groups={{0,1,2,3,4,5,6,7},{8,9,10,11,12,13,14,15},{16,17,18,19,20,21,22,23},{24..., dimensions={0} | all-to-all | bytes 4194304 | tf_op jit(solution)/shard_map/all_to_all | solution.py:180
  512.7 7.8 %shard_map.73 = (bf16[2,128,4096]{2,1,0:T(8,128)(2,1)}, bf16[2,128,4096]{2,1,0:T(8,128)(2,1)}, bf16[2,128,4096]{2,1,0:T(8,128)(2,1)}) custom-call(bf16[8,1,128,512]{3,2,1,0:T(8,128)(2,1)} %copy-done.2, bf16[8,1,128,512]{3,2,1,0:T(8,128)(2,1)} %copy-done.1, bf16[8,2,128,512]{3,2,1,0:T(8,128)(2,1)} %all_to_all.40.refs_2_, bf16[8,2,128,512]{3,2,1,0:T(8,128)(2,1)} %copy-done), custom_call_target="tpu_custom_call" | custom-call | tf_op jit(solution)/shard_map/pallas_call | solution.py:161
  (10 shorter events, 0.0 us)
Async XLA Ops:
  6.4 28.2 %all-to-all-start.3 = ((bf16[8,2,128,512]{3,2,1,0:T(8,128)(2,1)}), bf16[8,2,128,512]{3,2,1,0:T(8,128)(2,1)S(1)}, u32[]{:S(2)}, u32[]{:S(2)}) async-start(bf16[8,2,128,512]{3,2,1,0:T(8,128)(2,1)} %shard_map.70), calls=%async_computation.3 | async-start | bytes 4194304 | tf_op jit(solution)/shard_map/all_to_all | solution.py:180
  34.6 12.0 %copy-start.4 = (bf16[8,2,128,512]{3,2,1,0:T(8,128)(2,1)}, bf16[8,2,128,512]{3,2,1,0:T(8,128)(2,1)S(1)}, u32[]{:S(2)}) copy-start(bf16[8,2,128,512]{3,2,1,0:T(8,128)(2,1)S(1)} %all-to-all-done.3.kv_ref) | copy-start | bytes 6291460
  34.6 30.0 %all-to-all-start.4 = ((bf16[8,2,128,512]{3,2,1,0:T(8,128)(2,1)}), bf16[8,2,128,512]{3,2,1,0:T(8,128)(2,1)}, u32[]{:S(2)}, u32[]{:S(2)}) async-start(bf16[8,2,128,512]{3,2,1,0:T(8,128)(2,1)} %shard_map.71), calls=%async_computation.4 | async-start | bytes 4194304 | tf_op jit(solution)/shard_map/all_to_all | solution.py:180
  64.7 29.2 %all-to-all-start = ((bf16[8,2,128,512]{3,2,1,0:T(8,128)(2,1)}), bf16[8,2,128,512]{3,2,1,0:T(8,128)(2,1)S(1)}, u32[]{:S(2)}, u32[]{:S(2)}) async-start(bf16[8,2,128,512]{3,2,1,0:T(8,128)(2,1)} %shard_map.67), calls=%async_computation | async-start | bytes 4194304 | tf_op jit(solution)/shard_map/all_to_all | solution.py:180
  93.9 11.8 %copy-start.3 = (bf16[8,2,128,512]{3,2,1,0:T(8,128)(2,1)}, bf16[8,2,128,512]{3,2,1,0:T(8,128)(2,1)S(1)}, u32[]{:S(2)}) copy-start(bf16[8,2,128,512]{3,2,1,0:T(8,128)(2,1)S(1)} %all-to-all-done.kv_ref) | copy-start | bytes 6291460
  93.9 162.3 %all-to-all-start.1 = ((bf16[8,2,128,512]{3,2,1,0:T(8,128)(2,1)}), bf16[8,2,128,512]{3,2,1,0:T(8,128)(2,1)}, u32[]{:S(2)}, u32[]{:S(2)}) async-start(bf16[8,2,128,512]{3,2,1,0:T(8,128)(2,1)} %shard_map.68), calls=%async_computation.1 | async-start | bytes 4194304 | tf_op jit(solution)/shard_map/all_to_all | solution.py:180
  100.2 139.1 %collective-permute-start.1 = (bf16[8,2,128,512]{3,2,1,0:T(8,128)(2,1)}, bf16[8,2,128,512]{3,2,1,0:T(8,128)(2,1)}, u32[]{:S(2)}, u32[]{:S(2)}) collective-permute-start(bf16[8,2,128,512]{3,2,1,0:T(8,128)(2,1)} %copy-done.4), channel_id=1, source_target_pairs={{0,8},{1,9},{2,10},{3,11},{4,12},{5,13},{6,14},{7,15},{16,24},{17,... | collective-permute-start | bytes 6291464 | tf_op jit(solution)/shard_map/ppermute | solution.py:187
  105.7 178.4 %collective-permute-start = (bf16[8,2,128,512]{3,2,1,0:T(8,128)(2,1)S(1)}, bf16[8,2,128,512]{3,2,1,0:T(8,128)(2,1)}, u32[]{:S(2)}, u32[]{:S(2)}) collective-permute-start(bf16[8,2,128,512]{3,2,1,0:T(8,128)(2,1)S(1)} %all-to-all-done.kv_ref), channel_id=1, source_target_pairs={{0,8},{1,9},{2,10},{3,11},{4,12},{5,13},{6,14},{7,15},{16,24},{17,... | collective-permute-start | bytes 6291464 | tf_op jit(solution)/shard_map/ppermute | solution.py:187
  256.2 44.8 %all-to-all-start.5 = ((bf16[8,1,128,512]{3,2,1,0:T(8,128)(2,1)}), bf16[8,1,128,512]{3,2,1,0:T(8,128)(2,1)S(1)}, u32[]{:S(2)}, u32[]{:S(2)}) async-start(bf16[8,1,128,512]{3,2,1,0:T(8,128)(2,1)} %get-tuple-element.10), calls=%async_computation.5 | async-start | bytes 2097152 | tf_op jit(solution)/shard_map/all_to_all | solution.py:180
  262.0 78.0 %collective-permute-start.3 = (bf16[8,2,128,512]{3,2,1,0:T(8,128)(2,1)}, bf16[8,2,128,512]{3,2,1,0:T(8,128)(2,1)}, u32[]{:S(2)}, u32[]{:S(2)}) collective-permute-start(bf16[8,2,128,512]{3,2,1,0:T(8,128)(2,1)} %get-tuple-element.14), channel_id=1, source_target_pairs={{8,0},{9,1},{10,2},{11,3},{12,4},{13,5},{14,6},{15,7},{24,16},{25,... | collective-permute-start | bytes 6291464 | tf_op jit(solution)/shard_map/ppermute | solution.py:190
  301.0 43.3 %copy-start.1 = (bf16[8,1,128,512]{3,2,1,0:T(8,128)(2,1)}, bf16[8,1,128,512]{3,2,1,0:T(8,128)(2,1)S(1)}, u32[]{:S(2)}) copy-start(bf16[8,1,128,512]{3,2,1,0:T(8,128)(2,1)S(1)} %all-to-all-done.5.refs_1_) | copy-start | bytes 3145732
  301.0 43.3 %all-to-all-start.2 = ((bf16[8,1,128,512]{3,2,1,0:T(8,128)(2,1)}), bf16[8,1,128,512]{3,2,1,0:T(8,128)(2,1)S(1)}, u32[]{:S(2)}, u32[]{:S(2)}) async-start(bf16[8,1,128,512]{3,2,1,0:T(8,128)(2,1)} %get-tuple-element.9), calls=%async_computation.2 | async-start | bytes 2097152 | tf_op jit(solution)/shard_map/all_to_all | solution.py:180
  344.2 1.0 copy-start.2
  345.2 110.6 %all-to-all-start.7 = ((bf16[8,2,128,512]{3,2,1,0:T(8,128)(2,1)}), bf16[8,2,128,512]{3,2,1,0:T(8,128)(2,1)S(1)}, u32[]{:S(2)}, u32[]{:S(2)}) async-start(bf16[8,2,128,512]{3,2,1,0:T(8,128)(2,1)} %add_convert_fusion), calls=%async_computation.7 | async-start | bytes 4194304 | tf_op jit(solution)/shard_map/all_to_all | solution.py:180
  384.6 67.7 %collective-permute-start.2 = (bf16[8,2,128,512]{3,2,1,0:T(8,128)(2,1)}, bf16[8,2,128,512]{3,2,1,0:T(8,128)(2,1)S(1)}, u32[]{:S(2)}, u32[]{:S(2)}) collective-permute-start(bf16[8,2,128,512]{3,2,1,0:T(8,128)(2,1)} %get-tuple-element.12), channel_id=1, source_target_pairs={{8,0},{9,1},{10,2},{11,3},{12,4},{13,5},{14,6},{15,7},{24,16},{25,... | collective-permute-start | bytes 6291464 | tf_op jit(solution)/shard_map/ppermute | solution.py:190
  455.8 56.8 %copy-start = (bf16[8,2,128,512]{3,2,1,0:T(8,128)(2,1)}, bf16[8,2,128,512]{3,2,1,0:T(8,128)(2,1)S(1)}, u32[]{:S(2)}) copy-start(bf16[8,2,128,512]{3,2,1,0:T(8,128)(2,1)S(1)} %all-to-all-done.7.refs_3_) | copy-start | bytes 6291460
